TPU v7x, 512 devices: a whole 4x4x16 slice. The times are simulated.
512 devices in a mesh: group: 8 (over x, core), dev: 64 (over z, y).
Axes of the slice: x: 4, y: 4, z: 16, core: 2. Of those that a mesh axis runs over, the one named last changes fastest.
Arguments:
- cam_jac: float32 [2, 9, 8, 262144], P(None, None, None, ('group', 'dev')), may hold values from -6 to 6
- lm_jac: float32 [2, 3, 8, 262144], P(None, None, None, ('group', 'dev')), may hold values from -6 to 6
- resid: float32 [2, 8, 262144], P(None, None, ('group', 'dev')), may hold values from -6 to 6
- cam_index: int32 [8, 262144], P(None, ('group', 'dev')), may hold values from 0 to 8191
Outputs:
- camera_step: float32 [9, 8192], P(None, 'dev')
- camera_residual: float32 [9, 8192], P(None, 'dev')
- landmark_step: float32 [3, 262144], P(None, ('group', 'dev'))
Inputs may be any that keep to these rules, and one draw needn't show every extreme that they name: `cam_index`: every observation names one of the 8192 cameras.
All inputs are finite; a program needn't handle non-finite values.
Results may differ from a plain program's by a relative error of at most 0.0003.
Values sent between devices are 32-bit elements; how exact they have to be, the bound alone decides.
A program may use at most 64 MiB of HBM per device.

v0:
```python
import jax
import jax.numpy as jnp
from jax import lax
from jax.sharding import PartitionSpec as P

CAM_DEV = 128
ITERS = 2
DAMPING = 1.0


def landmark_inverse(lm_jac):

    def entry(first, second):
        return jnp.sum(lm_jac[:, first] * lm_jac[:, second], axis=(0, 1))

    w_00 = entry(0, 0) + DAMPING
    w_11 = entry(1, 1) + DAMPING
    w_22 = entry(2, 2) + DAMPING
    w_01 = entry(0, 1)
    w_02 = entry(0, 2)
    w_12 = entry(1, 2)
    cof_00 = w_11 * w_22 - w_12 * w_12
    cof_01 = w_02 * w_12 - w_01 * w_22
    cof_02 = w_01 * w_12 - w_02 * w_11
    cof_11 = w_00 * w_22 - w_02 * w_02
    cof_12 = w_01 * w_02 - w_00 * w_12
    cof_22 = w_00 * w_11 - w_01 * w_01
    determinant = w_00 * cof_00 + w_01 * cof_01 + w_02 * cof_02
    rows = [
        jnp.stack([cof_00, cof_01, cof_02]),
        jnp.stack([cof_01, cof_11, cof_12]),
        jnp.stack([cof_02, cof_12, cof_22]),
    ]
    return jnp.stack(rows) / determinant[None, None]


def apply_inverse(inverse, vector):
    return jnp.sum(inverse * vector[None], axis=1)


def landmark_side(lm_jac, values):
    return jnp.sum(lm_jac * values[:, None], axis=(0, 2))


def back_project(lm_jac, landmark):
    return jnp.sum(lm_jac * landmark[None, :, None, :], axis=1)


def camera_apply(cam_jac, cam_values):
    return jnp.sum(cam_jac * cam_values[None], axis=1)


def camera_transpose(cam_jac, errors):
    return jnp.sum(cam_jac * errors[:, None], axis=0)


def to_cameras(values, cam_index, total_cams):
    flat_index = cam_index.reshape(-1)
    width = values.shape[0]

    def one_row(column):
        return jax.ops.segment_sum(column, flat_index, num_segments=total_cams)

    return jax.vmap(one_row)(values.reshape(width, -1))


def schur_obs(cam_jac, lm_jac, inverse, cam_values):
    applied = camera_apply(cam_jac, cam_values)
    landmark = apply_inverse(inverse, landmark_side(lm_jac, applied))
    return camera_transpose(cam_jac, applied - back_project(lm_jac, landmark))


def gather_cameras(tile):
    return lax.all_gather(tile, "dev", axis=1, tiled=True)


def reduce_cameras(terms):
    totals = lax.psum(terms, ("group", "dev"))
    width = terms.shape[1] // lax.axis_size("dev")
    return lax.dynamic_slice_in_dim(totals, lax.axis_index("dev") * width, width, 1)


def inner_product(left, right):
    return lax.psum(jnp.sum(left * right), "dev")


def body(cam_jac, lm_jac, resid, cam_index):
    total_cams = CAM_DEV * lax.axis_size("dev")
    inverse = landmark_inverse(lm_jac)
    land_rhs = apply_inverse(inverse, landmark_side(lm_jac, resid))
    errors = resid - back_project(lm_jac, land_rhs)
    stacked = jnp.concatenate(
        [camera_transpose(cam_jac, errors), jnp.sum(cam_jac * cam_jac, axis=0)], axis=0
    )
    summed = reduce_cameras(to_cameras(stacked, cam_index, total_cams))
    gradient = summed[:9]
    diagonal = summed[9:] + DAMPING
    residual = gradient
    precond = residual / diagonal
    direction = precond
    rz_now = inner_product(residual, precond)
    solution = jnp.zeros_like(gradient)
    for iteration in range(ITERS):
        whole = gather_cameras(direction)
        cam_values = jnp.take(whole, cam_index, axis=1)
        terms = to_cameras(schur_obs(cam_jac, lm_jac, inverse, cam_values), cam_index, total_cams)
        image = reduce_cameras(terms) + DAMPING * direction
        alpha = rz_now / inner_product(direction, image)
        solution = solution + alpha * direction
        residual = residual - alpha * image
        if iteration + 1 < ITERS:
            precond = residual / diagonal
            rz_next = inner_product(residual, precond)
            direction = precond + rz_next / rz_now * direction
            rz_now = rz_next
    whole_step = gather_cameras(solution)
    cam_obs = camera_apply(cam_jac, jnp.take(whole_step, cam_index, axis=1))
    landmark_step = land_rhs - apply_inverse(inverse, landmark_side(lm_jac, cam_obs))
    return (solution, residual, landmark_step)


def solution(mesh):
    in_specs = (
        P(None, None, None, ("group", "dev")),
        P(None, None, None, ("group", "dev")),
        P(None, None, ("group", "dev")),
        P(None, ("group", "dev")),
    )
    out_specs = (P(None, "dev"), P(None, "dev"), P(None, ("group", "dev")))
    return jax.shard_map(body, mesh=mesh, in_specs=in_specs, out_specs=out_specs, check_vma=False)
```

profile of v0, /device:TPU:8, one launch (start us, length us, event | category | flops | bytes accessed | tf_op | source)
XLA Modules:
  0.0 2390.0 jit_solution(14837299796872105308)
XLA Ops:
  7.2 0.8 multiply_reduce_fusion.22
  8.0 0.9 multiply_reduce_fusion.13
  9.0 0.7 copy.31
  9.8 0.9 multiply_reduce_fusion.12
  10.7 0.8 sub.128
  11.5 1.0 multiply_reduce_fusion.6
  13.2 24.5 %scatter_custom_fusion = f32[18,8192]{0,1:T(8,128)} fusion(s32[4096]{0:T(1024)S(1)} %bitcast.43, f32[4096,18]{1,0:T(8,128)S(1)} %bitcast.38, f32[]{:T(128)} %constant.14.clone.1), kind=kCustom, calls=%fused_computation.13 | custom fusion | flops 73728 | bytes 589828 | tf_op jit(solution)/shard_map/vmap()/scatter-add | solution.py:62
  37.9 494.2 %all-reduce.5.cloned.1.call-done = f32[18,8192]{0,1:T(8,128)} async-done(((f32[18,8192]{0,1:T(8,128)}), f32[18,8192]{0,1:T(8,128)}) %all-reduce.5.cloned.1.call-update) | async-done | bytes 589840 | tf_op jit(solution)/shard_map/psum | solution.py:78
  532.1 1.0 fusion.7
  533.1 111.9 %all_gather.9 = f32[9,8192]{0,1:T(8,128)} all-gather(f32[9,128]{0,1:T(8,128)S(1)} %fusion.7), channel_id=1, replica_groups=mesh['group'=8,'dev'=64] {'dev'}, dimensions={1}, use_global_device_ids=true | all-gather | bytes 299520 | tf_op jit(solution)/shard_map/all_gather | solution.py:74
  645.0 16.3 gather_fusion
  661.3 1.9 select_bitcast_fusion.2
  664.8 24.5 %scatter_custom_fusion.1 = f32[9,8192]{0,1:T(8,128)} fusion(s32[4096]{0:T(1024)S(1)} %bitcast.44, f32[4096,9]{1,0:T(8,128)S(1)} %bitcast.40, f32[]{:T(128)} %constant.14.clone.1), kind=kCustom, calls=%fused_computation.11 | custom fusion | flops 36864 | bytes 294916 | tf_op jit(solution)/shard_map/vmap()/scatter-add | solution.py:62
  689.4 488.0 %all-reduce.7.cloned.1.call-done = f32[9,8192]{0,1:T(8,128)} async-done(((f32[9,8192]{0,1:T(8,128)}), f32[9,8192]{0,1:T(8,128)}) %all-reduce.7.cloned.1.call-update) | async-done | bytes 294928 | tf_op jit(solution)/shard_map/psum | solution.py:78
  1177.4 1.6 multiply_reduce_fusion.16
  1179.0 139.5 %all-reduce = (f32[]{:T(128)}, f32[]{:T(128)}) all-reduce(f32[]{:T(128)} %get-tuple-element.22, f32[]{:T(128)} %get-tuple-element.21), channel_id=1, replica_groups=mesh['group'=8,'dev'=64] {'dev'}, use_global_device_ids=true, to_apply=%region_14.0 | all-reduce | flops 2 | bytes 16 | tf_op jit(solution)/shard_map/psum | solution.py:84
  1319.8 1.6 multiply_reduce_fusion.15
  1321.4 140.7 %psum.53 = f32[]{:T(128)} all-reduce(f32[]{:T(128)} %get-tuple-element.25), channel_id=1, replica_groups=mesh['group'=8,'dev'=64] {'dev'}, use_global_device_ids=true, to_apply=%region_25.27 | all-reduce | flops 1 | bytes 8 | tf_op jit(solution)/shard_map/psum | solution.py:84
  1463.5 1.0 multiply_add_fusion.1
  1464.5 110.5 %all_gather.10 = f32[9,8192]{0,1:T(8,128)} all-gather(f32[9,128]{0,1:T(8,128)S(1)} %multiply_add_fusion.1), channel_id=1, replica_groups=mesh['group'=8,'dev'=64] {'dev'}, dimensions={1}, use_global_device_ids=true | all-gather | bytes 299520 | tf_op jit(solution)/shard_map/all_gather | solution.py:74
  1575.0 16.3 gather_fusion.1
  1591.2 1.9 select_bitcast_fusion.1
  1594.6 24.5 %scatter_custom_fusion.2 = f32[9,8192]{0,1:T(8,128)} fusion(s32[4096]{0:T(1024)S(1)} %bitcast.45, f32[4096,9]{1,0:T(8,128)S(1)} %bitcast.39, f32[]{:T(128)} %constant.14.clone.1), kind=kCustom, calls=%fused_computation.9 | custom fusion | flops 36864 | bytes 294916 | tf_op jit(solution)/shard_map/vmap()/scatter-add | solution.py:62
  1619.2 488.2 %all-reduce.9.cloned.1.call-done = f32[9,8192]{0,1:T(8,128)} async-done(((f32[9,8192]{0,1:T(8,128)}), f32[9,8192]{0,1:T(8,128)}) %all-reduce.9.cloned.1.call-update) | async-done | bytes 294928 | tf_op jit(solution)/shard_map/psum | solution.py:78
  2107.4 1.5 multiply_reduce_fusion.14
  2108.9 139.4 %psum.55 = f32[]{:T(128)} all-reduce(f32[]{:T(128)} %multiply_reduce_fusion.14), channel_id=1, replica_groups=mesh['group'=8,'dev'=64] {'dev'}, use_global_device_ids=true, to_apply=%region_34.36 | all-reduce | flops 1 | bytes 8 | tf_op jit(solution)/shard_map/psum | solution.py:84
  2249.7 1.0 multiply_subtract_fusion
  2250.7 0.7 copy.26
  2251.4 111.8 %all_gather.11 = f32[9,8192]{0,1:T(8,128)} all-gather(f32[9,128]{0,1:T(8,128)S(1)} %get-tuple-element.34), channel_id=1, replica_groups=mesh['group'=8,'dev'=64] {'dev'}, dimensions={1}, use_global_device_ids=true | all-gather | bytes 299520 | tf_op jit(solution)/shard_map/all_gather | solution.py:74
  2363.2 0.7 copy.27
  2363.9 16.3 gather_fusion.2
  2380.2 1.9 select_bitcast_fusion
  (42 shorter events, 5.1 us)
Async XLA Ops:
  7.2 524.9 %all-reduce.5.cloned.1.call-start = ((), (), s32[]{:S(2)}) async-start(), calls=%async_computation | async-start | bytes 8388608 | tf_op jit(solution)/shard_map/psum | solution.py:78
  13.2 24.6 %copy-start.2 = (s32[8,512]{1,0:T(8,128)S(1)}, s32[8,512]{1,0:T(8,128)}, u32[]{:S(2)}) copy-start(s32[8,512]{1,0:T(8,128)} %param.9) | copy-start | bytes 49156
  37.8 1139.6 %all-reduce.7.cloned.1.call-start = ((), (), s32[]{:S(2)}) async-start(), calls=%async_computation.1 | async-start | bytes 8388608 | tf_op jit(solution)/shard_map/psum | solution.py:78
  645.0 18.9 copy-start
  645.0 19.0 copy-start.1
  689.3 1418.1 %all-reduce.9.cloned.1.call-start = ((), (), s32[]{:S(2)}) async-start(), calls=%async_computation.2 | async-start | bytes 8388608 | tf_op jit(solution)/shard_map/psum | solution.py:78
Sparse Core Ops, SparseCore 0:
  37.9 494.1 all-reduce.4
  689.4 487.8 all-reduce.6
  1619.3 488.0 all-reduce.8
where the time goes:
time: 2390 us
  waiting for transfers between devices  1470 us (62%)
  blocking collectives  754 us (32%)
  other arithmetic  92.8 us (4%)
  local copies, waits for them, and re-layouts  54.8 us (2%)
    psum x3, waiting for transfers between devices, reduce_cameras(): totals = lax.psum(terms, ('group', 'dev'))  1470 us
    psum x3, blocking collectives, inner_product(): return lax.psum(jnp.sum(left * right), 'dev')  420 us
    all_gather x3, blocking collectives, gather_cameras(): return lax.all_gather(tile, 'dev', axis=1, tiled=True)  334 us
    scatter-add x3, other arithmetic, one_row(): return jax.ops.segment_sum(column, flat_index, num_segments=total_cams)  73.6 us
  transfers between devices with their start and end apart: 3, of which 3 were waited for; matrix products, arithmetic and copies ran while one was open for 0% of the time, Pallas kernels for 0%

commit v1 on v0

--- a/solution.py
+++ b/solution.py
@@ -75,7 +75,9 @@
 
 
 def reduce_cameras(terms):
-    totals = lax.psum(terms, ("group", "dev"))
+    totals = terms
+    for axis in ("group", "dev"):
+        totals = lax.psum(totals, axis)
     width = terms.shape[1] // lax.axis_size("dev")
     return lax.dynamic_slice_in_dim(totals, lax.axis_index("dev") * width, width, 1)
 

time: 2390 us -> 2060 us (0.86)
  the two profiles are of different devices: /device:TPU:8 before, /device:TPU:2 now
where the time goes in v1:
time: 2060 us
  waiting for transfers between devices  1140 us (55%)
  blocking collectives  754 us (37%)
  other arithmetic  92.7 us (4%)
  local copies, waits for them, and re-layouts  54.8 us (3%)
    psum x6, waiting for transfers between devices, reduce_cameras(): totals = lax.psum(totals, axis)  1140 us
    psum x3, blocking collectives, inner_product(): return lax.psum(jnp.sum(left * right), 'dev')  421 us
    all_gather x3, blocking collectives, gather_cameras(): return lax.all_gather(tile, 'dev', axis=1, tiled=True)  334 us
    scatter-add x3, other arithmetic, one_row(): return jax.ops.segment_sum(column, flat_index, num_segments=total_cams)  73.6 us
  transfers between devices with their start and end apart: 6, of which 6 were waited for; matrix products, arithmetic and copies ran while one was open for 0% of the time, Pallas kernels for 0%

profile of v1, /device:TPU:2, one launch (start us, length us, event | category | flops | bytes accessed | tf_op | source)
XLA Modules:
  0.0 2061.2 jit_solution(17571016680688022028)
XLA Ops:
  7.2 0.8 multiply_reduce_fusion.22
  8.0 0.9 multiply_reduce_fusion.13
  9.8 0.9 multiply_reduce_fusion.12
  10.7 0.8 sub.128
  11.5 1.0 multiply_reduce_fusion.6
  13.2 24.5 %scatter_custom_fusion = f32[18,8192]{0,1:T(8,128)} fusion(s32[4096]{0:T(1024)S(1)} %bitcast.43, f32[4096,18]{1,0:T(8,128)S(1)} %bitcast.38, f32[]{:T(128)} %constant.14.clone.1), kind=kCustom, calls=%fused_computation.13 | custom fusion | flops 73728 | bytes 589828 | tf_op jit(solution)/shard_map/vmap()/scatter-add | solution.py:62
  37.8 90.0 %all-reduce.8.cloned.1.call-done = f32[18,8192]{0,1:T(8,128)} async-done(((f32[18,8192]{0,1:T(8,128)}), f32[18,8192]{0,1:T(8,128)}) %all-reduce.8.cloned.1.call-update) | async-done | bytes 589840 | tf_op jit(solution)/shard_map/psum | solution.py:80
  127.9 296.3 %all-reduce.10.cloned.1.call-done = f32[18,8192]{0,1:T(8,128)} async-done(((f32[18,8192]{0,1:T(8,128)}), f32[18,8192]{0,1:T(8,128)}) %all-reduce.10.cloned.1.call-update) | async-done | bytes 589840 | tf_op jit(solution)/shard_map/psum | solution.py:80
  424.1 1.0 fusion.7
  425.1 111.5 %all_gather.9 = f32[9,8192]{0,1:T(8,128)} all-gather(f32[9,128]{0,1:T(8,128)S(1)} %fusion.7), channel_id=1, replica_groups=mesh['group'=8,'dev'=64] {'dev'}, dimensions={1}, use_global_device_ids=true | all-gather | bytes 299520 | tf_op jit(solution)/shard_map/all_gather | solution.py:74
  536.7 16.3 gather_fusion
  553.0 1.9 select_bitcast_fusion.2
  556.4 24.5 %scatter_custom_fusion.1 = f32[9,8192]{0,1:T(8,128)} fusion(s32[4096]{0:T(1024)S(1)} %bitcast.44, f32[4096,9]{1,0:T(8,128)S(1)} %bitcast.40, f32[]{:T(128)} %constant.14.clone.1), kind=kCustom, calls=%fused_computation.11 | custom fusion | flops 36864 | bytes 294916 | tf_op jit(solution)/shard_map/vmap()/scatter-add | solution.py:62
  581.0 80.9 %all-reduce.12.cloned.1.call-done = f32[9,8192]{0,1:T(8,128)} async-done(((f32[9,8192]{0,1:T(8,128)}), f32[9,8192]{0,1:T(8,128)}) %all-reduce.12.cloned.1.call-update) | async-done | bytes 294928 | tf_op jit(solution)/shard_map/psum | solution.py:80
  662.0 296.4 %all-reduce.14.cloned.1.call-done = f32[9,8192]{0,1:T(8,128)} async-done(((f32[9,8192]{0,1:T(8,128)}), f32[9,8192]{0,1:T(8,128)}) %all-reduce.14.cloned.1.call-update) | async-done | bytes 294928 | tf_op jit(solution)/shard_map/psum | solution.py:80
  958.4 1.6 multiply_reduce_fusion.16
  960.1 141.1 %all-reduce = (f32[]{:T(128)}, f32[]{:T(128)}) all-reduce(f32[]{:T(128)} %get-tuple-element.22, f32[]{:T(128)} %get-tuple-element.21), channel_id=1, replica_groups=mesh['group'=8,'dev'=64] {'dev'}, use_global_device_ids=true, to_apply=%region_15.0 | all-reduce | flops 2 | bytes 16 | tf_op jit(solution)/shard_map/psum | solution.py:86
  1102.5 1.6 multiply_reduce_fusion.15
  1104.1 138.8 %psum.76 = f32[]{:T(128)} all-reduce(f32[]{:T(128)} %get-tuple-element.25), channel_id=1, replica_groups=mesh['group'=8,'dev'=64] {'dev'}, use_global_device_ids=true, to_apply=%region_27.29 | all-reduce | flops 1 | bytes 8 | tf_op jit(solution)/shard_map/psum | solution.py:86
  1244.3 1.0 multiply_add_fusion.1
  1245.3 111.7 %all_gather.10 = f32[9,8192]{0,1:T(8,128)} all-gather(f32[9,128]{0,1:T(8,128)S(1)} %multiply_add_fusion.1), channel_id=1, replica_groups=mesh['group'=8,'dev'=64] {'dev'}, dimensions={1}, use_global_device_ids=true | all-gather | bytes 299520 | tf_op jit(solution)/shard_map/all_gather | solution.py:74
  1357.0 16.3 gather_fusion.1
  1373.3 1.9 select_bitcast_fusion.1
  1376.7 24.5 %scatter_custom_fusion.2 = f32[9,8192]{0,1:T(8,128)} fusion(s32[4096]{0:T(1024)S(1)} %bitcast.45, f32[4096,9]{1,0:T(8,128)S(1)} %bitcast.39, f32[]{:T(128)} %constant.14.clone.1), kind=kCustom, calls=%fused_computation.9 | custom fusion | flops 36864 | bytes 294916 | tf_op jit(solution)/shard_map/vmap()/scatter-add | solution.py:62
  1401.3 80.5 %all-reduce.16.cloned.1.call-done = f32[9,8192]{0,1:T(8,128)} async-done(((f32[9,8192]{0,1:T(8,128)}), f32[9,8192]{0,1:T(8,128)}) %all-reduce.16.cloned.1.call-update) | async-done | bytes 294928 | tf_op jit(solution)/shard_map/psum | solution.py:80
  1481.8 296.5 %all-reduce.18.cloned.1.call-done = f32[9,8192]{0,1:T(8,128)} async-done(((f32[9,8192]{0,1:T(8,128)}), f32[9,8192]{0,1:T(8,128)}) %all-reduce.18.cloned.1.call-update) | async-done | bytes 294928 | tf_op jit(solution)/shard_map/psum | solution.py:80
  1778.3 1.5 multiply_reduce_fusion.14
  1779.7 141.1 %psum.79 = f32[]{:T(128)} all-reduce(f32[]{:T(128)} %multiply_reduce_fusion.14), channel_id=1, replica_groups=mesh['group'=8,'dev'=64] {'dev'}, use_global_device_ids=true, to_apply=%region_37.39 | all-reduce | flops 1 | bytes 8 | tf_op jit(solution)/shard_map/psum | solution.py:86
  1922.2 1.0 multiply_subtract_fusion
  1923.9 110.3 %all_gather.11 = f32[9,8192]{0,1:T(8,128)} all-gather(f32[9,128]{0,1:T(8,128)S(1)} %get-tuple-element.34), channel_id=1, replica_groups=mesh['group'=8,'dev'=64] {'dev'}, dimensions={1}, use_global_device_ids=true | all-gather | bytes 299520 | tf_op jit(solution)/shard_map/all_gather | solution.py:74
  2034.8 16.3 gather_fusion.2
  2051.1 1.9 select_bitcast_fusion
  (51 shorter events, 7.3 us)
Async XLA Ops:
  7.2 120.6 %all-reduce.8.cloned.1.call-start = ((), (), s32[]{:S(2)}) async-start(), calls=%async_computation | async-start | bytes 8388608 | tf_op jit(solution)/shard_map/psum | solution.py:80
  37.7 90.1 %copy-start.2 = (s32[8,512]{1,0:T(8,128)S(1)}, s32[8,512]{1,0:T(8,128)}, u32[]{:S(2)}) copy-start(s32[8,512]{1,0:T(8,128)} %param.9) | copy-start | bytes 49156
  37.7 386.4 %all-reduce.10.cloned.1.call-start = ((), (), s32[]{:S(2)}) async-start(), calls=%async_computation.1 | async-start | bytes 8388608 | tf_op jit(solution)/shard_map/psum | solution.py:80
  127.7 534.2 %all-reduce.12.cloned.1.call-start = ((), (), s32[]{:S(2)}) async-start(), calls=%async_computation.2 | async-start | bytes 8388608 | tf_op jit(solution)/shard_map/psum | solution.py:80
  536.7 18.9 copy-start
  536.7 19.0 copy-start.1
  581.0 377.4 %all-reduce.14.cloned.1.call-start = ((), (), s32[]{:S(2)}) async-start(), calls=%async_computation.3 | async-start | bytes 8388608 | tf_op jit(solution)/shard_map/psum | solution.py:80
  661.9 819.8 %all-reduce.16.cloned.1.call-start = ((), (), s32[]{:S(2)}) async-start(), calls=%async_computation.4 | async-start | bytes 8388608 | tf_op jit(solution)/shard_map/psum | solution.py:80
  1401.3 377.0 %all-reduce.18.cloned.1.call-start = ((), (), s32[]{:S(2)}) async-start(), calls=%async_computation.5 | async-start | bytes 8388608 | tf_op jit(solution)/shard_map/psum | solution.py:80
Sparse Core Ops, SparseCore 0:
  37.8 89.8 all-reduce.7
  131.2 292.8 all-reduce.9
  581.1 80.7 all-reduce.11
  665.3 293.0 all-reduce.13
  1401.4 80.3 all-reduce.15
  1485.2 293.0 all-reduce.17
